TPU v7x, 32 devices: a whole 2x2x4 slice. The times are simulated.
32 devices in a mesh: dp: 32 (over z, y, x, core).
Axes of the slice: x: 2, y: 2, z: 4, core: 2. Of those that a mesh axis runs over, the one named last changes fastest.
Arguments:
- tokens: bfloat16 [32768, 768], P('dp'), may hold values from -6 to 6
- lengths: int32 [64], P('dp'), may hold values from 16 to 512, as said below
- groups: int32 [64], replicated, may hold values from 0 to 63, as said below
- query_weight: bfloat16 [768, 768], replicated, may hold values from -0.21875 to 0.21875
- query_bias: float32 [768], replicated, may hold values from -1.2 to 1.2
- key_weight: bfloat16 [768, 768], replicated, may hold values from -0.21875 to 0.21875
- value_weight: bfloat16 [768, 768], replicated, may hold values from -0.21875 to 0.21875
- value_bias: float32 [768], replicated, may hold values from -1.2 to 1.2
- output_weight: bfloat16 [768, 768], replicated, may hold values from -1.25 to 1.25
- output_bias: float32 [768], replicated, may hold values from -1.2 to 1.2
- first_gain: float32 [768], replicated, may hold values from 0.5 to 1.5
- first_shift: float32 [768], replicated, may hold values from -1.2 to 1.2
- inner_weight: bfloat16 [768, 3072], replicated, may hold values from -0.21875 to 0.21875
- inner_bias: float32 [3072], replicated, may hold values from -1.2 to 1.2
- outer_weight: bfloat16 [3072, 768], replicated, may hold values from -0.109375 to 0.109375
- outer_bias: float32 [768], replicated, may hold values from -1.2 to 1.2
- second_gain: float32 [768], replicated, may hold values from 0.5 to 1.5
- second_shift: float32 [768], replicated, may hold values from -1.2 to 1.2
Outputs:
- loss: float32 [], replicated
- layer_output: bfloat16 [32768, 768], P('dp')
- token_grad: float32 [32768, 768], P('dp')
- query_weight_grad: float32 [768, 768], P('dp')
- query_bias_grad: float32 [768], P('dp')
- key_weight_grad: float32 [768, 768], P('dp')
- value_weight_grad: float32 [768, 768], P('dp')
- value_bias_grad: float32 [768], P('dp')
- output_weight_grad: float32 [768, 768], P('dp')
- output_bias_grad: float32 [768], P('dp')
- first_gain_grad: float32 [768], P('dp')
- first_shift_grad: float32 [768], P('dp')
- inner_weight_grad: float32 [768, 3072], P('dp')
- inner_bias_grad: float32 [3072], P('dp')
- outer_weight_grad: float32 [3072, 768], P('dp')
- outer_bias_grad: float32 [768], P('dp')
- second_gain_grad: float32 [768], P('dp')
- second_shift_grad: float32 [768], P('dp')
Inputs may be any that keep to these rules, and one draw needn't show every extreme that they name: The 2 sentences of one device come from one length bucket: bucket b holds lengths from b * 128 + 1 (at least 16) to (b + 1) * 128; in every draw one sentence has exactly 512 tokens. `groups`: sentences with equal numbers form a group of 1 to 6 sentences; some group has exactly 6.
All inputs are finite; a program needn't handle non-finite values.
Results may differ from a plain program's by a relative error of at most 0.014.
Values may be sent and summed in bfloat16 or wider, within the bound.
A program may use at most 192 MiB of HBM per device.

v0:
```python
import math

import jax
import jax.numpy as jnp
from jax import lax
from jax.sharding import PartitionSpec as P

HEADS = 12
HD = 64


cosine_scale = 20.0
layer_epsilon = 1e-06
unit_epsilon = 1e-06
highest = lax.Precision.HIGHEST


def project(operand, weight):
    return jnp.dot(operand, weight, preferred_element_type=jnp.float32)


def transpose_left(left_rows, right_rows):
    return lax.dot_general(
        left_rows, right_rows, (((0,), (0,)), ((), ())), preferred_element_type=jnp.float32
    )


def transpose_right(operand, weight):
    return lax.dot_general(
        operand, weight, (((1,), (1,)), ((), ())), preferred_element_type=jnp.float32
    )


def standardize(residual):
    center = residual - jnp.mean(residual, axis=-1, keepdims=True)
    inverse = lax.rsqrt(jnp.mean(center * center, axis=-1, keepdims=True) + layer_epsilon)
    return (center * inverse, inverse)


def standardize_back(upstream, normed, inverse, scaling):
    scaled = upstream * scaling
    return inverse * (
        scaled
        - jnp.mean(scaled, axis=-1, keepdims=True)
        - normed * jnp.mean(scaled * normed, axis=-1, keepdims=True)
    )


def gelu_slope(inner_pre):
    cumulative = 0.5 * (1.0 + lax.erf(inner_pre * (1.0 / math.sqrt(2.0))))
    density = jnp.exp(-0.5 * inner_pre * inner_pre) * (1.0 / math.sqrt(2.0 * math.pi))
    return cumulative + inner_pre * density


def masked_scores(queries, key_rows, key_live):
    scores = jnp.einsum("qhd,khd->hqk", queries, key_rows, preferred_element_type=jnp.float32)
    return jnp.where(key_live[None, None, :], scores, -1e30)


def attend(pieces):
    queries, key_rows, value_rows, key_live = pieces
    scores = masked_scores(queries, key_rows, key_live)
    summit = jnp.max(scores, axis=-1, keepdims=True)
    raised = jnp.exp(scores - summit)
    totals = jnp.sum(raised, axis=-1, keepdims=True)
    weights = (raised / totals).astype(jnp.bfloat16)
    mixture = jnp.einsum("hqk,khd->qhd", weights, value_rows, preferred_element_type=jnp.float32)
    return (mixture.astype(jnp.bfloat16), (summit + jnp.log(totals))[..., 0])


def attend_back(pieces):
    queries, key_rows, value_rows, key_live, log_total, upstream = pieces
    scores = masked_scores(queries, key_rows, key_live)
    chances = jnp.exp(scores - log_total[..., None])
    toward = jnp.einsum("qhd,khd->hqk", upstream, value_rows, preferred_element_type=jnp.float32)
    score_grad = (chances * (toward - jnp.sum(chances * toward, axis=-1, keepdims=True))).astype(
        jnp.bfloat16
    )
    value_grad = jnp.einsum(
        "hqk,qhd->khd", chances.astype(jnp.bfloat16), upstream, preferred_element_type=jnp.float32
    )
    query_grad = jnp.einsum(
        "hqk,khd->qhd", score_grad, key_rows, preferred_element_type=jnp.float32
    )
    key_grad = jnp.einsum("hqk,qhd->khd", score_grad, queries, preferred_element_type=jnp.float32)
    return (
        query_grad.astype(jnp.bfloat16),
        key_grad.astype(jnp.bfloat16),
        value_grad.astype(jnp.bfloat16),
    )


def contrast_rows(row_unit, unit_rows, row_groups, groups, row_start):
    similar = cosine_scale * lax.dot_general(
        row_unit, unit_rows, (((1,), (1,)), ((), ())), precision=highest
    )
    row_ids = row_start + jnp.arange(row_unit.shape[0])
    column_ids = jnp.arange(unit_rows.shape[0])
    itself = row_ids[:, None] == column_ids[None, :]
    logits = jnp.where(itself, -1e30, similar)
    summit = jnp.max(logits, axis=-1, keepdims=True)
    raised = jnp.exp(logits - summit)
    totals = jnp.sum(raised, axis=-1, keepdims=True)
    chances = raised / totals
    log_total = summit + jnp.log(totals)
    matched = jnp.logical_and(
        row_groups[:, None] == groups[None, :], jnp.logical_not(itself)
    ).astype(jnp.float32)
    weights = matched / jnp.maximum(jnp.sum(matched, axis=-1, keepdims=True), 1.0)
    row_mass = jnp.sum(weights, axis=-1, keepdims=True)
    loss_rows = row_mass[:, 0] * log_total[:, 0] - jnp.sum(weights * similar, axis=-1)
    return (jnp.sum(loss_rows), row_mass * chances - weights)


def per_device(
    tokens,
    lengths,
    groups,
    query_weight,
    query_bias,
    key_weight,
    value_weight,
    value_bias,
    output_weight,
    output_bias,
    first_gain,
    first_shift,
    inner_weight,
    inner_bias,
    outer_weight,
    outer_bias,
    second_gain,
    second_shift,
):
    seq_count = lengths.shape[0]
    slot_count = tokens.shape[0] // seq_count
    model_width = tokens.shape[1]
    heads_shape = (seq_count, slot_count, HEADS, HD)
    queries = ((project(tokens, query_weight) + query_bias) * 0.125).astype(jnp.bfloat16)
    key_rows = project(tokens, key_weight).astype(jnp.bfloat16)
    value_rows = (project(tokens, value_weight) + value_bias).astype(jnp.bfloat16)
    key_live = jnp.arange(slot_count)[None, :] < lengths[:, None]
    head_queries = queries.reshape(heads_shape)
    head_keys = key_rows.reshape(heads_shape)
    head_values = value_rows.reshape(heads_shape)
    mixture, log_total = lax.map(attend, (head_queries, head_keys, head_values, key_live))
    mixture = mixture.reshape(tokens.shape)
    first_normed, first_inverse = standardize(
        tokens.astype(jnp.float32) + project(mixture, output_weight) + output_bias
    )
    hidden = first_normed * first_gain + first_shift
    hidden_low = hidden.astype(jnp.bfloat16)
    inner_pre = project(hidden_low, inner_weight) + inner_bias
    activated = jax.nn.gelu(inner_pre, approximate=False).astype(jnp.bfloat16)
    second_normed, second_inverse = standardize(
        hidden + project(activated, outer_weight) + outer_bias
    )
    output = second_normed * second_gain + second_shift
    live_rows = key_live.astype(jnp.float32)[:, :, None]
    counts = lengths.astype(jnp.float32)[:, None]
    pooled = (
        jnp.sum(output.reshape(seq_count, slot_count, model_width) * live_rows, axis=1) / counts
    ).astype(jnp.bfloat16)
    everyone = lax.all_gather(pooled, "dp", axis=0, tiled=True).astype(jnp.float32)
    inverse_all = lax.rsqrt(jnp.sum(everyone * everyone, axis=-1, keepdims=True) + unit_epsilon)
    unit_rows = everyone * inverse_all
    first_row = lax.axis_index("dp") * seq_count
    own_unit = lax.dynamic_slice_in_dim(unit_rows, first_row, seq_count, 0)
    own_inverse = lax.dynamic_slice_in_dim(inverse_all, first_row, seq_count, 0)
    own_groups = lax.dynamic_slice_in_dim(groups, first_row, seq_count, 0)
    part_loss, coupling = contrast_rows(own_unit, unit_rows, own_groups, groups, first_row)
    loss_value = lax.psum(part_loss, "dp")
    spread = cosine_scale * lax.dot_general(
        coupling, own_unit, (((0,), (0,)), ((), ())), precision=highest
    )
    unit_grad = cosine_scale * jnp.dot(coupling, unit_rows, precision=highest) + lax.psum_scatter(
        spread, "dp", scatter_dimension=0, tiled=True
    )
    pooled_grad = own_inverse * (
        unit_grad - own_unit * jnp.sum(own_unit * unit_grad, axis=-1, keepdims=True)
    )
    grad_output = (pooled_grad[:, None, :] / counts[:, :, None] * live_rows).reshape(tokens.shape)
    second_gain_grad = jnp.sum(grad_output * second_normed, axis=0)
    second_shift_grad = jnp.sum(grad_output, axis=0)
    grad_second = standardize_back(grad_output, second_normed, second_inverse, second_gain)
    branch_grad = grad_second.astype(jnp.bfloat16)
    outer_bias_grad = jnp.sum(branch_grad, axis=0, dtype=jnp.float32)
    outer_weight_grad = transpose_left(activated, branch_grad)
    inner_grad = (transpose_right(branch_grad, outer_weight) * gelu_slope(inner_pre)).astype(
        jnp.bfloat16
    )
    inner_bias_grad = jnp.sum(inner_grad, axis=0, dtype=jnp.float32)
    inner_weight_grad = transpose_left(hidden_low, inner_grad)
    hidden_grad = grad_second + transpose_right(inner_grad, inner_weight)
    first_gain_grad = jnp.sum(hidden_grad * first_normed, axis=0)
    first_shift_grad = jnp.sum(hidden_grad, axis=0)
    grad_first = standardize_back(hidden_grad, first_normed, first_inverse, first_gain)
    attended_grad = grad_first.astype(jnp.bfloat16)
    output_bias_grad = jnp.sum(attended_grad, axis=0, dtype=jnp.float32)
    output_weight_grad = transpose_left(mixture, attended_grad)
    mixture_grad = transpose_right(attended_grad, output_weight).astype(jnp.bfloat16)
    query_grad, key_grad, value_grad = lax.map(
        attend_back,
        (
            head_queries,
            head_keys,
            head_values,
            key_live,
            log_total,
            mixture_grad.reshape(heads_shape),
        ),
    )
    query_grad = query_grad.reshape(tokens.shape)
    key_grad = key_grad.reshape(tokens.shape)
    value_grad = value_grad.reshape(tokens.shape)
    query_weight_grad = 0.125 * transpose_left(tokens, query_grad)
    query_bias_grad = 0.125 * jnp.sum(query_grad, axis=0, dtype=jnp.float32)
    key_weight_grad = transpose_left(tokens, key_grad)
    value_weight_grad = transpose_left(tokens, value_grad)
    value_bias_grad = jnp.sum(value_grad, axis=0, dtype=jnp.float32)
    token_grad = (
        grad_first
        + 0.125 * transpose_right(query_grad, query_weight)
        + transpose_right(key_grad, key_weight)
        + transpose_right(value_grad, value_weight)
    )
    summed = tuple(
        (
            lax.psum_scatter(query_weight_grad, "dp", scatter_dimension=0, tiled=True),
            lax.psum_scatter(query_bias_grad, "dp", scatter_dimension=0, tiled=True),
            lax.psum_scatter(key_weight_grad, "dp", scatter_dimension=0, tiled=True),
            lax.psum_scatter(value_weight_grad, "dp", scatter_dimension=0, tiled=True),
            lax.psum_scatter(value_bias_grad, "dp", scatter_dimension=0, tiled=True),
            lax.psum_scatter(output_weight_grad, "dp", scatter_dimension=0, tiled=True),
            lax.psum_scatter(output_bias_grad, "dp", scatter_dimension=0, tiled=True),
            lax.psum_scatter(first_gain_grad, "dp", scatter_dimension=0, tiled=True),
            lax.psum_scatter(first_shift_grad, "dp", scatter_dimension=0, tiled=True),
            lax.psum_scatter(inner_weight_grad, "dp", scatter_dimension=0, tiled=True),
            lax.psum_scatter(inner_bias_grad, "dp", scatter_dimension=0, tiled=True),
            lax.psum_scatter(outer_weight_grad, "dp", scatter_dimension=0, tiled=True),
            lax.psum_scatter(outer_bias_grad, "dp", scatter_dimension=0, tiled=True),
            lax.psum_scatter(second_gain_grad, "dp", scatter_dimension=0, tiled=True),
            lax.psum_scatter(second_shift_grad, "dp", scatter_dimension=0, tiled=True),
        )
    )
    return (loss_value, output.astype(jnp.bfloat16), token_grad) + summed


def solution(mesh):
    placed = (
        P("dp", None),
        P("dp"),
        P(),
        P(),
        P(),
        P(),
        P(),
        P(),
        P(),
        P(),
        P(),
        P(),
        P(),
        P(),
        P(),
        P(),
        P(),
        P(),
    )
    return jax.shard_map(
        per_device,
        mesh=mesh,
        in_specs=placed,
        out_specs=(
            P(),
            P("dp", None),
            P("dp", None),
            P("dp", None),
            P("dp"),
            P("dp", None),
            P("dp", None),
            P("dp"),
            P("dp", None),
            P("dp"),
            P("dp"),
            P("dp"),
            P("dp", None),
            P("dp"),
            P("dp", None),
            P("dp"),
            P("dp"),
            P("dp"),
        ),
        check_vma=False,
    )
```

profile of v0, /device:TPU:0, one launch (start us, length us, event | category | flops | bytes accessed | tf_op | source)
XLA Modules:
  0.0 1026.4 jit_solution(14815421118209120909)
XLA Ops:
  11.9 4.3 multiply_convert_fusion.1
  27.7 3.8 reshape.237
  39.7 3.8 reshape.239
  47.8 19.2 %while.26 = (s32[]{:T(128)}, bf16[2,512,12,64]{1,3,2,0:T(8,128)(2,1)}, f32[2,12,512]{2,1,0:T(8,128)S(1)}, bf16[2,512,12,64]{1,3,2,0:T(8,128)(2,1)}, pred[2,512]{...) while((s32[]{:T(128)}, ...), condition=%wide.region_5.6_spmd, body=%wide.region_2.0_spmd.sunk | while | flops 834004992 | bytes 47428224 | solution.py:146
  75.6 34.8 %fusion.58 = (bf16[1024,3072]{1,0:T(8,128)(2,1)S(1)}, f32[1024,3072]{1,0:T(8,128)}) fusion(f32[3072]{0:T(1024)S(1)} %copy-done.77, bf16[768,3072]{1,0:T(8,128)(2,1)S(1)} %bitcast.221, f32[1024,768]{1,0:T(8,128)S(1)} %get-tuple-element.293, f32[768]{0:T(1024)S(1)} %copy-done.42, f32[768]{0:T(1024)S(1)} %copy-done.39, f32[1024]{0:T(1024)S(1)} %add_rsqrt_fusion.1, ...), kind=kOutput, calls=%fused_computation.65 | convolution fusion | flops 5043388416 | bytes 26765312 | tf_op jit(solution)/shard_map/dot_general | solution.py:19
  110.5 5.4 fusion.106
  119.1 43.5 %all-gather = bf16[32,2,768]{2,1,0:T(2,128)(2,1)S(1)} all-gather(bf16[1,2,768]{2,1,0:T(2,128)(2,1)S(1)} %fusion.84), channel_id=1, replica_groups=mesh['dp'=32] {'dp'}, dimensions={0}, use_global_device_ids=true | all-gather | bytes 101376 | tf_op jit(solution)/shard_map/all_gather | solution.py:164
  165.3 119.1 %all-reduce.13.cloned.1.call-done = f32[64,768]{1,0:T(8,128)} async-done(((f32[64,768]{1,0:T(8,128)}), f32[64,768]{1,0:T(8,128)}) %all-reduce.13.cloned.1.call-update) | async-done | bytes 196624
  292.4 13.0 %convert_reduce_fusion = (f32[3072]{0:T(1024)}, bf16[1024,3072]{1,0:T(8,128)(2,1)S(1)}) fusion(f32[1024,3072]{1,0:T(8,128)} %get-tuple-element.295, f32[3072]{0:T(1024)S(1)} %copy-done.77, bf16[1024,768]{1,0:T(8,128)(2,1)S(1)} %get-tuple-element.278, bf16[3072,768]{1,0:T(8,128)(2,1)} %param.36), kind=kOutput, calls=%fused_computation.72 | convolution fusion | flops 4872729600 | bytes 25190400 | tf_op jit(solution)/shard_map/dot_general | solution.py:29
  305.5 6.6 multiply_reduce_fusion.2
  318.5 4.5 convolution_convert_fusion.2
  334.3 49.2 %while.27 = (s32[]{:T(128)}, bf16[2,512,12,64]{1,3,2,0:T(8,128)(2,1)}, bf16[2,512,12,64]{1,3,2,0:T(8,128)(2,1)}, bf16[2,512,12,64]{1,3,2,0:T(8,128)(2,1)}, bf16[...) while((s32[]{:T(128)}, ...), condition=%wide.region_25.26_spmd, body=%wide.region_23.25_spmd.sunk | while | flops 2052188160 | bytes 159055760 | solution.py:202
  340.3 6.7 multiply_reduce_fusion.12
  347.0 7.2 multiply_convert_fusion.3
  364.7 6.6 multiply_reduce_fusion.12
  371.3 7.4 multiply_convert_fusion.3
  414.5 10.1 fusion.109
  425.3 11.2 %fusion.97 = f32[768,3072]{1,0:T(8,128)} fusion(bf16[1024,3072]{1,0:T(8,128)(2,1)} %copy-done.19, f32[1024,768]{1,0:T(8,128)} %copy-done.7, f32[768]{0:T(1024)S(1)} %copy-done.43, f32[768]{0:T(1024)S(1)} %copy-done.40, f32[1024]{0:T(1024)S(1)} %copy-done.36, f32[1024]{0:T(1024)S(1)} %copy-done.34), kind=kOutput, calls=%fused_computation.170 | convolution fusion | flops 4835770368 | bytes 18888704 | tf_op jit(solution)/shard_map/dot_general | solution.py:23
  440.0 41.8 %all-reduce.10 = (f32[]{:T(128)}, f32[768]{0:T(1024)S(1)}, f32[768]{0:T(1024)S(1)}, f32[768]{0:T(1024)S(1)}, f32[768]{0:T(1024)S(1)}, /*index=5*/f32[768]{0:T(10...) all-reduce(f32[]{:T(128)} %subtract_reduce_fusion, ...), channel_id=1, replica_groups=mesh['dp'=32] {'dp'}, use_global_device_ids=true, to_apply=%region_16.17 | all-reduce | flops 9217 | bytes 73736 | tf_op jit(solution)/shard_map/psum | solution.py:172
  496.3 31.6 %reduce-scatter.19.cloned.1.call-done = f32[24,768]{1,0:T(8,128)} async-done(((f32[768,768]{1,0:T(8,128)}), f32[24,768]{1,0:T(8,128)}) %reduce-scatter.19.cloned.1.call-update) | async-done | bytes 73744
  527.9 103.8 %reduce-scatter.23.cloned.1.call-done = f32[24,768]{1,0:T(8,128)} async-done(((f32[768,768]{1,0:T(8,128)}), f32[24,768]{1,0:T(8,128)}) %reduce-scatter.23.cloned.1.call-update) | async-done | bytes 73744
  631.7 104.6 %reduce-scatter.21.cloned.1.call-done = f32[24,768]{1,0:T(8,128)} async-done(((f32[768,768]{1,0:T(8,128)}), f32[24,768]{1,0:T(8,128)}) %reduce-scatter.21.cloned.1.call-update) | async-done | bytes 73744
  736.3 140.8 %reduce-scatter.17.cloned.1.call-done = f32[96,768]{1,0:T(8,128)} async-done(((f32[3072,768]{1,0:T(8,128)}), f32[96,768]{1,0:T(8,128)}) %reduce-scatter.17.cloned.1.call-update) | async-done | bytes 294928 | tf_op jit(solution)/shard_map/reduce_scatter | solution.py:240
  877.1 142.3 %reduce-scatter.15.cloned.1.call-done = f32[24,3072]{1,0:T(8,128)} async-done(((f32[768,3072]{1,0:T(8,128)}), f32[24,3072]{1,0:T(8,128)}) %reduce-scatter.15.cloned.1.call-update) | async-done | bytes 294928 | tf_op jit(solution)/shard_map/reduce_scatter | solution.py:238
  (321 shorter events, 157.4 us)
Async XLA Ops:
  7.2 64.0 %copy-start = (bf16[768,768]{1,0:T(8,128)(2,1)S(1)}, bf16[768,768]{1,0:T(8,128)(2,1)}, u32[]{:S(2)}) copy-start(bf16[768,768]{1,0:T(8,128)(2,1)} %param.30) | copy-start | bytes 3538948
  7.2 277.2 %all-reduce.13.cloned.1.call-start = ((), (), s32[]{:S(2)}) async-start(), calls=%async_computation.12 | async-start | bytes 393216
  71.2 39.2 %slice-start = ((s8[4718592]{0:T(1024)(128)(4,1)}), s8[4194304]{0:T(1024)(128)(4,1)S(1)}, s32[]{:S(2)}) async-start(s8[4718592]{0:T(1024)(128)(4,1)} %bitcast.218), calls=%async_computation.13 | async-start | bytes 8388608
  72.9 37.5 %copy-start.7 = (f32[1024,768]{1,0:T(8,128)}, f32[1024,768]{1,0:T(8,128)S(1)}, u32[]{:S(2)}) copy-start(f32[1024,768]{1,0:T(8,128)S(1)} %get-tuple-element.293) | copy-start | bytes 9437188
  72.9 239.2 %copy-start.33 = (f32[1024]{0:T(1024)}, f32[1024]{0:T(1024)S(1)}, u32[]{:S(2)}) copy-start(f32[1024]{0:T(1024)S(1)} %broadcast_multiply_fusion.6) | copy-start | bytes 12292
  75.6 236.5 %copy-start.35 = (f32[1024]{0:T(1024)}, f32[1024]{0:T(1024)S(1)}, u32[]{:S(2)}) copy-start(f32[1024]{0:T(1024)S(1)} %add_rsqrt_fusion.1) | copy-start | bytes 12292
  75.6 34.9 %slice-start.1 = ((s8[4718592]{0:T(1024)(128)(4,1)}), s8[524288]{0:T(1024)(128)(4,1)S(1)}, s32[]{:S(2)}) async-start(s8[4718592]{0:T(1024)(128)(4,1)} %bitcast.218), calls=%async_computation.14 | async-start | bytes 1048576
  75.6 34.9 %copy-start.80 = (f32[768]{0:T(1024)S(1)}, f32[768]{0:T(1024)}, u32[]{:S(2)}) copy-start(f32[768]{0:T(1024)} %param.37) | copy-start | bytes 9220
  118.4 44.5 %copy-start.58 = (s32[2]{0:T(128)S(1)}, s32[2]{0:T(128)}, u32[]{:S(2)}) copy-start(s32[2]{0:T(128)} %copy-done.57) | copy-start | bytes 28
  118.4 44.5 %copy-start.63 = (s32[64]{0:T(128)S(1)}, s32[64]{0:T(128)}, u32[]{:S(2)}) copy-start(s32[64]{0:T(128)} %param.24) | copy-start | bytes 772
  118.4 44.5 %copy-start.65 = (s32[2]{0:T(128)S(1)}, s32[2]{0:T(128)}, u32[]{:S(2)}) copy-start(s32[2]{0:T(128)} %copy-done.64) | copy-start | bytes 28
  118.4 44.5 %copy-start.67 = (f32[2]{0:T(128)S(1)}, f32[2]{0:T(128)}, u32[]{:S(2)}) copy-start(f32[2]{0:T(128)} %broadcast_maximum_fusion) | copy-start | bytes 28
  118.4 46.9 %copy-start.49 = (f32[1,4,2,128]{3,2,1,0:T(2,128)S(1)}, f32[1,4,2,128]{3,2,1,0:T(2,128)}, u32[]{:S(2)}) copy-start(f32[1,4,2,128]{3,2,1,0:T(2,128)} %get-tuple-element.289) | copy-start | bytes 12292
  163.8 123.1 %copy-start.51 = (f32[2]{0:T(128)}, f32[2]{0:T(128)S(1)}, u32[]{:S(2)}) copy-start(f32[2]{0:T(128)S(1)} %get-tuple-element.230) | copy-start | bytes 28
  164.0 128.4 %copy-start.53 = (f32[2]{0:T(128)}, f32[2]{0:T(128)S(1)}, u32[]{:S(2)}) copy-start(f32[2]{0:T(128)S(1)} %get-tuple-element.281) | copy-start | bytes 28
  165.2 331.2 %reduce-scatter.13.cloned.1.call-start = ((), (), s32[]{:S(2)}) async-start(), calls=%async_computation.6 | async-start | bytes 2433024 | tf_op jit(solution)/shard_map/reduce_scatter | solution.py:234
  290.4 15.0 %slice-start.4 = ((s8[4718592]{0:T(1024)(128)(4,1)}), s8[4194304]{0:T(1024)(128)(4,1)S(1)}, s32[]{:S(2)}) async-start(s8[4718592]{0:T(1024)(128)(4,1)} %bitcast.222), calls=%async_computation.17 | async-start | bytes 8388608
  292.4 13.1 %slice-start.5 = ((s8[4718592]{0:T(1024)(128)(4,1)}), s8[524288]{0:T(1024)(128)(4,1)S(1)}, s32[]{:S(2)}) async-start(s8[4718592]{0:T(1024)(128)(4,1)} %bitcast.222), calls=%async_computation.18 | async-start | bytes 1048576
  323.0 204.9 %reduce-scatter.19.cloned.1.call-start = ((), (), s32[]{:S(2)}) async-start(), calls=%async_computation.9 | async-start | bytes 2433024
  394.4 237.3 %reduce-scatter.23.cloned.1.call-start = ((), (), s32[]{:S(2)}) async-start(), calls=%async_computation.11 | async-start | bytes 2433024
  403.6 332.7 %reduce-scatter.21.cloned.1.call-start = ((), (), s32[]{:S(2)}) async-start(), calls=%async_computation.10 | async-start | bytes 2433024
  414.5 462.6 %reduce-scatter.17.cloned.1.call-start = ((), (), s32[]{:S(2)}) async-start(), calls=%async_computation.8 | async-start | bytes 9732096 | tf_op jit(solution)/shard_map/reduce_scatter | solution.py:240
  424.6 594.8 %reduce-scatter.15.cloned.1.call-start = ((), (), s32[]{:S(2)}) async-start(), calls=%async_computation.7 | async-start | bytes 9732096 | tf_op jit(solution)/shard_map/reduce_scatter | solution.py:238
  493.1 526.3 %copy-start.1 = (bf16[768,768]{1,0:T(8,128)(2,1)S(1)}, bf16[768,768]{1,0:T(8,128)(2,1)}, u32[]{:S(2)}) copy-start(bf16[768,768]{1,0:T(8,128)(2,1)} %param.30) | copy-start | bytes 3538948
  (81 other events, 252.7 us)
Sparse Core Ops, SparseCore 0:
  165.3 119.0 all-reduce.12
  323.1 99.9 reduce-scatter.12
  429.8 98.0 reduce-scatter.18
  533.6 98.0 reduce-scatter.22
  638.3 97.9 reduce-scatter.20
  742.6 134.4 reduce-scatter.16
  884.6 134.8 reduce-scatter.14
where the time goes:
time: 1030 us
  waiting for transfers between devices  642 us (62%)
  matrix products  165 us (16%)
  blocking collectives  85.2 us (8%)
  local copies, waits for them, and re-layouts  79.8 us (8%)
  other arithmetic  37.5 us (4%)
  between operations  15.2 us (1%)
    unnamed x11, waiting for transfers between devices  359 us
    reduce_scatter x1, waiting for transfers between devices, per_device(): lax.psum_scatter(inner_weight_grad, 'dp', scatter_dimension=0, tiled=True)  142 us
    reduce_scatter x1, waiting for transfers between devices, per_device(): lax.psum_scatter(outer_weight_grad, 'dp', scatter_dimension=0, tiled=True)  141 us
    dot_general x6, matrix products, project(): return jnp.dot(operand, weight, preferred_element_type=jnp.float32)  51.3 us
    all_gather x1, blocking collectives, per_device(): lax.all_gather(pooled, 'dp', axis=0, tiled=True).astype(jnp.float32)  43.5 us
    psum x1, blocking collectives, per_device(): loss_value = lax.psum(part_loss, 'dp')  41.8 us
    dot_general x6, matrix products, transpose_left(): lax.dot_general(left_rows, right_rows, (((0,), (0,)), ((), ())), preferre...  32.6 us
    dot_general x6, matrix products, transpose_right(): lax.dot_general(operand, weight, (((1,), (1,)), ((), ())), preferred_elem...  32.1 us
  transfers between devices with their start and end apart: 7, of which 6 were waited for; matrix products, arithmetic and copies ran while one was open for 12% of the time, Pallas kernels for 0%

commit v1 on v0

--- a/solution.py
+++ b/solution.py
@@ -1,17 +1,1278 @@
+import functools
 import math
 
 import jax
 import jax.numpy as jnp
 from jax import lax
+from jax.experimental import pallas as pl
+from jax.experimental.pallas import tpu as pltpu
 from jax.sharding import PartitionSpec as P
 
 HEADS = 12
 HD = 64
-
-
 cosine_scale = 20.0
 layer_epsilon = 1e-06
 unit_epsilon = 1e-06
+low = jnp.bfloat16
+full = jnp.float32
+MIB = 1 << 20
+
+
+def dot(left, right, left_axis=1, right_axis=0):
+    return lax.dot_general(
+        left, right, (((left_axis,), (right_axis,)), ((), ())), preferred_element_type=full
+    )
+
+
+def gelu_pair(value):
+    size = jnp.abs(value)
+    ratio = pl.reciprocal(1.0 + (0.3275911 / math.sqrt(2.0)) * size, approx=True)
+    bell = jnp.exp(value * value * -0.5)
+    series = 0.5 * 1.061405429
+    for factor in (-1.453152027, 1.421413741, -0.284496736, 0.254829592):
+        series = series * ratio + 0.5 * factor
+    half_tail = series * ratio * bell
+    cumulative = jnp.where(value >= 0.0, 1.0 - half_tail, half_tail)
+    return value * cumulative, cumulative + value * bell * (1.0 / math.sqrt(2.0 * math.pi))
+
+
+def spread_lanes(column, lanes=128):
+    return jnp.broadcast_to(column, (column.shape[0], lanes))
+
+
+def forward_kernel(
+    lengths,
+    tokens,
+    vectors,
+    inner_bias,
+    query_weight,
+    key_weight,
+    value_weight,
+    output_weight,
+    inner_weight,
+    outer_weight,
+    layer_output,
+    pooled,
+    live_mean,
+    queries_t,
+    keys_t,
+    values,
+    mixture_t,
+    probs,
+    inverse_totals,
+    first_normed,
+    first_inverse,
+    hidden_low,
+    second_normed,
+    second_inverse,
+    activated,
+    slopes,
+    tokens_t,
+    w_query,
+    w_key,
+    w_value,
+    w_output,
+    w_inner,
+    w_outer,
+    key_rows,
+    values_t,
+    mask_block,
+    raised,
+    total_second,
+    hidden_full,
+    sems,
+    raised_sems,
+):
+    sentence = pl.program_id(0)
+    slots, width = tokens.shape
+    parts = activated.shape[0]
+    part = activated.shape[2]
+    length = lengths[sentence]
+    weights = (
+        (query_weight, w_query),
+        (key_weight, w_key),
+        (value_weight, w_value),
+        (output_weight, w_output),
+        (inner_weight, w_inner),
+        (outer_weight, w_outer),
+    )
+    copies = [
+        pltpu.make_async_copy(source, target, sems.at[place])
+        for place, (source, target) in enumerate(weights)
+    ]
+
+    @pl.when(sentence == 0)
+    def _():
+        for copy in copies:
+            copy.start()
+
+    slot_ids = lax.broadcasted_iota(jnp.int32, (slots, 128), 0)
+    lane_ids = lax.broadcasted_iota(jnp.int32, (slots, 128), 1)
+    mask_block[...] = jnp.where(
+        jnp.logical_and(slot_ids >= length, lane_ids == 0), -1e30, 0.0
+    ).astype(low)
+
+    def ready(place):
+        @pl.when(sentence == 0)
+        def _():
+            copies[place].wait()
+
+    block = tokens[...]
+    tokens_t[...] = block.T
+    ready(0)
+    queries_t[...] = ((dot(block, w_query[...]) + vectors[0:1, :]) * 0.125).astype(low).T
+    ready(1)
+    rows = dot(block, w_key[...]).astype(low)
+    key_rows[...] = rows
+    keys_t[...] = rows.T
+    ready(2)
+    rows = (dot(block, w_value[...]) + vectors[1:2, :]).astype(low)
+    values[...] = rows
+    values_t[...] = rows.T
+
+    pick_row = jnp.where(
+        lax.broadcasted_iota(jnp.int32, (128, slots), 0) == 0, 1.0, 0.0
+    ).astype(low)
+    empty = jnp.zeros((HD, slots), low)
+    depth = raised.shape[0]
+
+    def raised_copy(head):
+        return pltpu.make_async_copy(
+            raised.at[lax.rem(head, depth)],
+            probs.at[sentence * HEADS + head],
+            raised_sems.at[lax.rem(head, depth)],
+        )
+
+    def head_pair(pair, carry):
+        start = pl.multiple_of(pair * 128, 128)
+        left = jnp.concatenate([key_rows[:, pl.ds(start, 128)], mask_block[...]], axis=1)
+        pair_queries = queries_t[pl.ds(start, 128), :]
+        for half in range(2):
+            head = pair * 2 + half
+            if half == 0:
+                right = jnp.concatenate([pair_queries[:HD], empty, pick_row], axis=0)
+            else:
+                right = jnp.concatenate([empty, pair_queries[HD:], pick_row], axis=0)
+
+            @pl.when(pair >= depth // 2)
+            def _():
+                raised_copy(head).wait()
+
+            scores = dot(left, right)
+            summit = jnp.max(scores, axis=0, keepdims=True)
+            totals = jnp.zeros((8, slots), full)
+            slot = lax.rem(head, depth)
+            step = 64
+            for place in range(0, slots, step):
+                piece = jnp.exp(scores[place : place + step, :] - summit)
+                totals = totals + jnp.sum(piece.reshape(step // 8, 8, slots), axis=0)
+                raised[slot, place : place + step, :] = piece.astype(low)
+            inverse = 1.0 / jnp.sum(totals, axis=0, keepdims=True)
+            raised_copy(head).start()
+            inverse_totals[head] = jnp.broadcast_to(inverse, (8, slots))
+            row = pl.multiple_of(start + half * HD, HD)
+            mixed = dot(values_t[pl.ds(row, HD), :], raised[slot]) * inverse
+            mixture_t[pl.ds(row, HD), :] = mixed.astype(low)
+        return carry
+
+    lax.fori_loop(0, HEADS // 2, head_pair, 0)
+
+    ready(3)
+    attended = dot(mixture_t[...], w_output[...], 0, 0)
+    step = 32
+    for place in range(0, slots, step):
+        rows = slice(place, place + step)
+        residual = block[rows].astype(full) + attended[rows] + vectors[2:3, :]
+        center = residual - jnp.mean(residual, axis=1, keepdims=True)
+        inverse = lax.rsqrt(jnp.mean(center * center, axis=1, keepdims=True) + layer_epsilon)
+        normed = center * inverse
+        hidden = normed * vectors[3:4, :] + vectors[4:5, :]
+        first_normed[rows, :] = normed
+        first_inverse[rows, :] = spread_lanes(inverse)
+        hidden_low[rows, :] = hidden.astype(low)
+        hidden_full[rows, :] = hidden
+
+    ready(4)
+    ready(5)
+    total_second[...] = jnp.zeros_like(total_second)
+
+    def feed(index, carry):
+        start = pl.multiple_of(index * part, part)
+        inner = dot(hidden_low[...], w_inner[:, pl.ds(start, part)])
+        offset = inner_bias[:, pl.ds(start, part)]
+        step = 32
+        for place in range(0, slots, step):
+            value, slope = gelu_pair(inner[place : place + step] + offset)
+            activated[index, place : place + step, :] = value.astype(low)
+            slopes[index, place : place + step, :] = slope.astype(low)
+        total_second[...] += dot(activated[index], w_outer[pl.ds(start, part), :])
+        return carry
+
+    lax.fori_loop(0, parts, feed, 0)
+
+    live_sum = jnp.zeros((8, width), full)
+    count = length.astype(full)
+    step = 32
+    for place in range(0, slots, step):
+        rows = slice(place, place + step)
+        residual = hidden_full[rows, :] + total_second[rows, :] + vectors[5:6, :]
+        center = residual - jnp.mean(residual, axis=1, keepdims=True)
+        inverse = lax.rsqrt(jnp.mean(center * center, axis=1, keepdims=True) + layer_epsilon)
+        normed = center * inverse
+        second_normed[rows, :] = normed
+        layer_output[rows, :] = (normed * vectors[6:7, :] + vectors[7:8, :]).astype(low)
+        live = lax.broadcasted_iota(jnp.int32, (step, width), 0) + place < length
+        live_sum = live_sum + jnp.sum(
+            jnp.where(live, normed, 0.0).reshape(step // 8, 8, width), axis=0
+        )
+        alive = lax.broadcasted_iota(jnp.int32, (step, 128), 0) + place < length
+        second_inverse[rows, :] = jnp.where(alive, spread_lanes(inverse) / count, 0.0)
+    mean_normed = jnp.sum(live_sum, axis=0, keepdims=True) / count
+    live_mean[0] = jnp.broadcast_to(mean_normed, (8, width))
+    vector = (mean_normed * vectors[6:7, :] + vectors[7:8, :]).astype(low).astype(full)
+    pooled[0] = jnp.broadcast_to(vector, (8, width))
+
+    for head in range(HEADS - depth, HEADS):
+        raised_copy(head).wait()
+
+
+def forward(lengths, tokens, vectors, inner_bias, weights):
+    count = lengths.shape[0]
+    rows, width = tokens.shape
+    slots = rows // count
+    inner = weights[4].shape[1]
+    part = 768
+    parts = inner // part
+    hbm = pl.BlockSpec(memory_space=pl.ANY)
+    vmem = pl.BlockSpec(memory_space=pltpu.VMEM)
+
+    def by_rows(columns):
+        return pl.BlockSpec((slots, columns), lambda s: (s, 0))
+
+    by_columns = pl.BlockSpec((width, slots), lambda s: (0, s))
+    by_sentence = pl.BlockSpec((1, 8, width), lambda s: (s, 0, 0))
+    by_parts = pl.BlockSpec((parts, slots, part), lambda s: (0, s, 0))
+    shape = jax.ShapeDtypeStruct
+    return pl.pallas_call(
+        forward_kernel,
+        grid=(count,),
+        in_specs=[pl.BlockSpec(memory_space=pltpu.SMEM), by_rows(width), vmem, vmem] + [hbm] * 6,
+        out_specs=[
+            by_rows(width),
+            by_sentence,
+            by_sentence,
+            by_columns,
+            by_columns,
+            by_rows(width),
+            by_columns,
+            hbm,
+            pl.BlockSpec((HEADS, 8, slots), lambda s: (s, 0, 0)),
+            by_rows(width),
+            by_rows(128),
+            by_rows(width),
+            by_rows(width),
+            by_rows(128),
+            by_parts,
+            by_parts,
+            by_columns,
+        ],
+        out_shape=[
+            shape((rows, width), low),
+            shape((count, 8, width), full),
+            shape((count, 8, width), full),
+            shape((width, rows), low),
+            shape((width, rows), low),
+            shape((rows, width), low),
+            shape((width, rows), low),
+            shape((count * HEADS, slots, slots), low),
+            shape((count * HEADS, 8, slots), full),
+            shape((rows, width), full),
+            shape((rows, 128), full),
+            shape((rows, width), low),
+            shape((rows, width), full),
+            shape((rows, 128), full),
+            shape((parts, rows, part), low),
+            shape((parts, rows, part), low),
+            shape((width, rows), low),
+        ],
+        scratch_shapes=[pltpu.VMEM(w.shape, low) for w in weights]
+        + [
+            pltpu.VMEM((slots, width), low),
+            pltpu.VMEM((width, slots), low),
+            pltpu.VMEM((slots, 128), low),
+            pltpu.VMEM((4, slots, slots), low),
+            pltpu.VMEM((slots, width), full),
+            pltpu.VMEM((slots, width), full),
+            pltpu.SemaphoreType.DMA((6,)),
+            pltpu.SemaphoreType.DMA((4,)),
+        ],
+        compiler_params=pltpu.CompilerParams(vmem_limit_bytes=62 * MIB),
+        name="encode",
+    )(lengths, tokens, vectors, inner_bias, *weights)
+
+
+def partner_of(me, mask):
+    bit = lax.rem(lax.div(me, mask), 2)
+    return bit, me + mask * (1 - 2 * bit)
+
+
+class Summation:
+    def __init__(self, buffers, sems, place, links):
+        self.send, self.held = buffers[0], buffers[1:]
+        self.send_sems, self.recv_sems = sems
+        self.place = place
+        self.links = links
+        self.third = self.held[0].shape[-2] // 3
+        self.started = []
+
+    def exchange(self, stage, part, source, target, link):
+        copy = pltpu.make_async_remote_copy(
+            src_ref=source,
+            dst_ref=target,
+            send_sem=self.send_sems.at[self.place, stage, part],
+            recv_sem=self.recv_sems.at[self.place, stage, part],
+            device_id=(self.links[link][1],),
+            device_id_type=pl.DeviceIdType.MESH,
+        )
+        return copy
+
+    def views(self, stage, away):
+        h = self.third
+
+        def side(link):
+            bit = self.links[link][0]
+            return 1 - bit if away else bit
+
+        if stage == 0:
+            return [self.send.at[:, :, :, :, side("core")]]
+        if stage == 1:
+            r = self.held[0]
+            return [
+                r.at[:, :, :, side("x"), pl.ds(0, h)],
+                r.at[:, :, side("y"), :, pl.ds(h, h)],
+                r.at[:, side("z0"), :, :, pl.ds(2 * h, h)],
+            ]
+        if stage == 2:
+            r = self.held[1]
+            return [r.at[0, :, :, side("y")], r.at[1, :, side("z0")], r.at[2, :, :, side("x")]]
+        if stage == 3:
+            r = self.held[2]
+            return [r.at[0, :, side("z0")], r.at[1, :, side("x")], r.at[2, :, side("y")]]
+        r = self.held[3]
+        return [r.at[part, side("z1")] for part in range(3)]
+
+    def copies(self, stage):
+        routes = (
+            ("core",),
+            ("x", "y", "z0"),
+            ("y", "z0", "x"),
+            ("z0", "x", "y"),
+            ("z1", "z1", "z1"),
+        )[stage]
+        sources = self.views(stage, True)
+        target = self.held[stage]
+        targets = [target] if stage == 0 else [target.at[part] for part in range(3)]
+        return [
+            self.exchange(stage, part, source, goal, link)
+            for part, (source, goal, link) in enumerate(zip(sources, targets, routes))
+        ]
+
+    def start(self, stage=0):
+        for copy in self.copies(stage):
+            copy.start()
+
+    def step(self, stage, out=None):
+        for copy in self.copies(stage):
+            copy.wait()
+        kept = self.views(stage, False)
+        if stage == 0:
+            self.held[0][...] = self.held[0][...] + kept[0][...]
+        elif stage < 4:
+            for part in range(3):
+                self.held[stage][part] = self.held[stage][part] + kept[part][...]
+        else:
+            h = self.third
+            for part in range(3):
+                out[part * h : part * h + h, :] = kept[part][...].astype(full) + self.held[4][
+                    part
+                ].astype(full)
+        if stage < 4:
+            self.start(stage + 1)
+
+
+def contrast(points, groups):
+    count = points.shape[0]
+    inverse = lax.rsqrt(jnp.sum(points * points, axis=1, keepdims=True) + unit_epsilon)
+    unit = points * inverse
+    similar = cosine_scale * lax.dot_general(
+        unit,
+        unit,
+        (((1,), (1,)), ((), ())),
+        precision=lax.Precision.HIGHEST,
+        preferred_element_type=full,
+    )
+    rows = lax.broadcasted_iota(jnp.int32, (count, count), 0)
+    columns = lax.broadcasted_iota(jnp.int32, (count, count), 1)
+    itself = rows == columns
+    logits = jnp.where(itself, -1e30, similar)
+    summit = jnp.max(logits, axis=1, keepdims=True)
+    raised = jnp.exp(logits - summit)
+    totals = jnp.sum(raised, axis=1, keepdims=True)
+    chances = raised / totals
+    log_total = summit + jnp.log(totals)
+    across = jnp.broadcast_to(groups, (count, count))
+    matched = jnp.where(
+        jnp.logical_and(across == across.T, jnp.logical_not(itself)), 1.0, 0.0
+    )
+    weights = matched / jnp.maximum(jnp.sum(matched, axis=1, keepdims=True), 1.0)
+    row_mass = jnp.sum(weights, axis=1, keepdims=True)
+    loss_rows = row_mass * log_total - jnp.sum(weights * similar, axis=1, keepdims=True)
+    loss = jnp.sum(loss_rows, axis=0, keepdims=True)
+    coupling = row_mass * chances - weights
+    unit_grad = cosine_scale * lax.dot_general(
+        coupling + coupling.T,
+        unit,
+        (((1,), (0,)), ((), ())),
+        precision=lax.Precision.HIGHEST,
+        preferred_element_type=full,
+    )
+    grad = inverse * (unit_grad - unit * jnp.sum(unit * unit_grad, axis=1, keepdims=True))
+    return loss, grad
+
+
+def backward_kernel(
+    devices,
+    sentences,
+    pooled,
+    live_mean,
+    vectors,
+    groups,
+    activated_in,
+    slopes_in,
+    second_normed_in,
+    second_inverse_in,
+    hidden_low_in,
+    first_normed_in,
+    first_inverse_in,
+    mixture_t_in,
+    queries_t_in,
+    keys_t_in,
+    values_in,
+    tokens_t_in,
+    probs_in,
+    inverse_totals_in,
+    query_weight,
+    key_weight,
+    value_weight,
+    output_weight,
+    inner_weight,
+    outer_weight,
+    loss_out,
+    token_grad_out,
+    outer_out,
+    inner_out,
+    square_out,
+    sums_out,
+    act,
+    inner_grad,
+    w_rows,
+    w_columns,
+    mixture_t,
+    normed,
+    grads,
+    branch,
+    hidden_low,
+    second_inverse,
+    first_inverse,
+    inverse_totals,
+    score_grads,
+    own,
+    gathered,
+    points,
+    outer_send,
+    outer_0,
+    outer_1,
+    outer_2,
+    outer_3,
+    outer_4,
+    inner_send,
+    inner_0,
+    inner_1,
+    inner_2,
+    inner_3,
+    inner_4,
+    square_0,
+    square_1,
+    square_2,
+    square_3,
+    square_4,
+    sum_held,
+    sum_recv,
+    load_sems,
+    prob_sems,
+    gather_send,
+    gather_recv,
+    set_send,
+    set_recv,
+    sum_send,
+    sum_sems,
+):
+    me = lax.axis_index("dp")
+    rows, width = normed.shape
+    slots = rows // sentences
+    parts = act.shape[0]
+    heads = width // HD
+    links = {
+        "core": partner_of(me, 1),
+        "x": partner_of(me, 2),
+        "y": partner_of(me, 4),
+        "z0": partner_of(me, 8),
+        "z1": partner_of(me, 16),
+    }
+    load_count = iter(range(64))
+
+    def load(source, target):
+        return pltpu.make_async_copy(source, target, load_sems.at[next(load_count)])
+
+    get_normed = load(second_normed_in, normed)
+    get_second = load(second_inverse_in, second_inverse)
+    get_act = load(activated_in, act)
+    get_outer = load(outer_weight, w_rows)
+    get_slopes = load(slopes_in, inner_grad)
+    get_hidden = load(hidden_low_in, hidden_low)
+    get_inner = load(inner_weight, w_columns)
+    get_first = load(first_inverse_in, first_inverse)
+    get_mixture = load(mixture_t_in, mixture_t)
+    get_totals = load(inverse_totals_in, inverse_totals)
+    early = (
+        get_normed,
+        get_second,
+        get_act,
+        get_outer,
+        get_slopes,
+        get_hidden,
+        get_inner,
+        get_first,
+        get_mixture,
+        get_totals,
+    )
+    for copy in early:
+        copy.start()
+
+    barrier = pltpu.get_barrier_semaphore()
+
+    def greet(step, carry):
+        other = lax.rem(me + step, devices)
+        pl.semaphore_signal(
+            barrier, inc=1, device_id=(other,), device_id_type=pl.DeviceIdType.MESH
+        )
+        return carry
+
+    lax.fori_loop(1, devices, greet, 0)
+    for sentence in range(sentences):
+        own[sentence : sentence + 1, :] = pooled[sentence, 0:1, :]
+    gathered[me] = own[...]
+    pl.semaphore_wait(barrier, devices - 1)
+
+    def gather_copy(step):
+        return pltpu.make_async_remote_copy(
+            src_ref=own,
+            dst_ref=gathered.at[me],
+            send_sem=gather_send.at[step],
+            recv_sem=gather_recv.at[step],
+            device_id=(lax.rem(me + step, devices),),
+            device_id_type=pl.DeviceIdType.MESH,
+        )
+
+    def gather_start(step, carry):
+        gather_copy(step).start()
+        return carry
+
+    def gather_wait(step, carry):
+        gather_copy(step).wait()
+        return carry
+
+    lax.fori_loop(1, devices, gather_start, 0)
+    lax.fori_loop(1, devices, gather_wait, 0)
+    for device in range(devices):
+        points[device * sentences : (device + 1) * sentences, :] = gathered[device]
+    loss, pooled_grad = contrast(points[...], groups[...])
+    loss_out[...] = jnp.broadcast_to(loss, loss_out.shape)
+    row_ids = lax.broadcasted_iota(jnp.int32, (devices * sentences, width), 0)
+    own_grads = [
+        jnp.sum(
+            jnp.where(row_ids == me * sentences + sentence, pooled_grad, 0.0),
+            axis=0,
+            keepdims=True,
+        )
+        for sentence in range(sentences)
+    ]
+    vector_sums = sum_held.at[0]
+    vector_sums[...] = jnp.zeros_like(vector_sums)
+    vector_sums[1:2, :] = sum(
+        own_grads[sentence] * live_mean[sentence, 0:1, :] for sentence in range(sentences)
+    )
+    vector_sums[2:3, :] = sum(own_grads)
+
+    outer_set = Summation(
+        (outer_send, outer_0, outer_1, outer_2, outer_3, outer_4), (set_send, set_recv), 0, links
+    )
+    inner_set = Summation(
+        (inner_send, inner_0, inner_1, inner_2, inner_3, inner_4), (set_send, set_recv), 1, links
+    )
+    piece_rows, piece_columns = outer_send.shape[-2] // 2, width // 2
+    square_sends = [
+        outer_send.at[
+            :,
+            :,
+            :,
+            :,
+            :,
+            pl.ds(place % 2 * piece_rows, piece_rows),
+            pl.ds(place // 2 * piece_columns, piece_columns),
+        ]
+        for place in range(4)
+    ]
+    square_sets = [
+        Summation(
+            (square_sends[place],)
+            + tuple(
+                ref.at[place] for ref in (square_0, square_1, square_2, square_3, square_4)
+            ),
+            (set_send, set_recv),
+            2 + place,
+            links,
+        )
+        for place in range(4)
+    ]
+
+    def widen(column, lanes=width):
+        return jnp.concatenate([column] * (lanes // 128), axis=1)
+
+    get_normed.wait()
+    get_second.wait()
+    bias_sum = jnp.zeros((8, width), full)
+    step = 32
+    for sentence in range(sentences):
+        scaled = own_grads[sentence] * vectors[6:7, :]
+        shifted = scaled - jnp.mean(scaled, axis=1, keepdims=True)
+
+        def second_back(index, total):
+            at = pl.ds(pl.multiple_of(sentence * slots + index * step, step), step)
+            unit = normed[at, :]
+            mass = jnp.mean(unit * scaled, axis=1, keepdims=True)
+            grad = widen(second_inverse[at, :]) * (shifted - unit * mass)
+            grads[at, :] = grad
+            rounded = grad.astype(low)
+            branch[at, :] = rounded
+            return total + jnp.sum(
+                rounded.astype(full).reshape(step // 8, 8, width), axis=0
+            )
+
+        bias_sum = lax.fori_loop(0, slots // step, second_back, bias_sum)
+    vector_sums[0:1, :] = jnp.sum(bias_sum, axis=0, keepdims=True)
+    get_normed_2 = load(first_normed_in, normed)
+    get_normed_2.start()
+
+    get_act.wait()
+
+    def cores_of(index):
+        return [(y, x, core) for y in range(2) for x in range(2) for core in range(2)][index]
+
+    def outer_block(index, carry):
+        result = dot(act[index], branch[...], 0, 0).astype(low)
+        high, below = lax.div(index, 2), lax.rem(index, 2)
+        piece = outer_send.shape[-2]
+        for place in range(8):
+            y, x, core = cores_of(place)
+            outer_send[high, below, y, x, core] = result[place * piece : (place + 1) * piece, :]
+        return carry
+
+    lax.fori_loop(0, parts, outer_block, 0)
+    outer_set.start()
+
+    get_values = load(values_in, act.at[0])
+    get_values.start()
+
+    def prob_slot(order):
+        place = lax.rem(order, 4)
+        return act.at[
+            2 + lax.div(place, 2),
+            pl.ds(pl.multiple_of(lax.rem(place, 2) * slots, slots), slots),
+            0:slots,
+        ]
+
+    def prob_copy(order):
+        half = lax.rem(order, 2)
+        sentence = lax.rem(lax.div(order, 2), sentences)
+        pair = lax.div(order, 2 * sentences)
+        return pltpu.make_async_copy(
+            probs_in.at[sentence * heads + pair * 2 + half],
+            prob_slot(order),
+            prob_sems.at[lax.rem(order, 4)],
+        )
+
+    for order in range(3):
+        prob_copy(order).start()
+
+    get_outer.wait()
+    get_slopes.wait()
+
+    def inner_block(index, carry):
+        start = pl.multiple_of(index * width, width)
+        weight = w_rows[pl.ds(start, width), :]
+        total = jnp.zeros((8, width), full)
+        for piece in range(2):
+            span = rows // 2
+            result = dot(branch[piece * span : (piece + 1) * span, :], weight, 1, 1)
+            for place in range(0, span, step):
+                at = pl.ds(piece * span + place, step)
+                value = (
+                    result[place : place + step] * inner_grad[index, at, :].astype(full)
+                ).astype(low)
+                inner_grad[index, at, :] = value
+                total = total + jnp.sum(
+                    value.astype(full).reshape(step // 8, 8, width), axis=0
+                )
+        vector_sums[pl.ds(8 + index, 1), :] = jnp.sum(total, axis=0, keepdims=True)
+        return carry
+
+    lax.fori_loop(0, parts, inner_block, 0)
+    square_loads = [
+        load(source, w_rows.at[pl.ds(place * width, width)])
+        for place, source in enumerate((output_weight, query_weight, key_weight, value_weight))
+    ]
+    for copy in square_loads:
+        copy.start()
+
+    outer_set.step(0)
+
+    get_hidden.wait()
+    own_rows = width // devices
+    for block in range(2):
+        left = hidden_low[:, block * (width // 2) : (block + 1) * (width // 2)].T
+
+        def inner_weight_block(index, carry):
+            upper = dot(left, inner_grad[index])
+            lower = dot(left, inner_grad[index + 2])
+            start = pl.multiple_of(index * width, width)
+            for place in range(16):
+                y, x, core = cores_of(place % 8)
+                at = slice(place * own_rows, (place + 1) * own_rows)
+                inner_send[block, place // 8, y, x, core, :, pl.ds(start, width)] = (
+                    jnp.concatenate([upper[at], lower[at]], axis=0).astype(low)
+                )
+            return carry
+
+        lax.fori_loop(0, 2, inner_weight_block, 0)
+    inner_set.start()
+
+    get_inner.wait()
+    get_normed_2.wait()
+    get_first.wait()
+    span = 256
+
+    def hidden_block(index, sums):
+        gain_sum, shift_sum, bias_sum = sums
+        base = pl.multiple_of(index * span, span)
+        total = dot(inner_grad[0, pl.ds(base, span), :], w_columns[:, 0:width], 1, 1)
+        for part in range(1, parts):
+            total = total + dot(
+                inner_grad[part, pl.ds(base, span), :],
+                w_columns[:, part * width : (part + 1) * width],
+                1,
+                1,
+            )
+        for place in range(0, span, step):
+            at = pl.ds(base + place, step)
+            upstream = grads[at, :] + total[place : place + step]
+            unit = normed[at, :]
+            gain_sum = gain_sum + jnp.sum((upstream * unit).reshape(step // 8, 8, width), axis=0)
+            shift_sum = shift_sum + jnp.sum(upstream.reshape(step // 8, 8, width), axis=0)
+            scaled = upstream * vectors[3:4, :]
+            center = scaled - jnp.mean(scaled, axis=1, keepdims=True)
+            grad = widen(first_inverse[at, :]) * (
+                center - unit * jnp.mean(scaled * unit, axis=1, keepdims=True)
+            )
+            grads[at, :] = grad
+            rounded = grad.astype(low)
+            branch[at, :] = rounded
+            bias_sum = bias_sum + jnp.sum(
+                rounded.astype(full).reshape(step // 8, 8, width), axis=0
+            )
+        return gain_sum, shift_sum, bias_sum
+
+    zero = jnp.zeros((8, width), full)
+    gain_sum, shift_sum, bias_sum = lax.fori_loop(
+        0, rows // span, hidden_block, (zero, zero, zero)
+    )
+    vector_sums[3:4, :] = jnp.sum(gain_sum, axis=0, keepdims=True)
+    vector_sums[4:5, :] = jnp.sum(shift_sum, axis=0, keepdims=True)
+    vector_sums[5:6, :] = jnp.sum(bias_sum, axis=0, keepdims=True)
+
+    get_queries = load(queries_t_in, w_columns.at[:, 0:rows])
+    get_keys = load(keys_t_in, w_columns.at[:, rows : 2 * rows])
+    get_queries.start()
+    get_keys.start()
+    get_tokens = [
+        load(
+            tokens_t_in.at[:, sentence * slots : (sentence + 1) * slots],
+            inner_grad.at[2 + sentence, 0:width, 0:slots],
+        )
+        for sentence in range(sentences)
+    ]
+    for copy in get_tokens:
+        copy.start()
+    outer_set.step(1)
+    inner_set.step(0)
+
+    def square_pieces(place, result):
+        half = width // 2
+        for device in range(devices):
+            y, x, core = cores_of(device % 8)
+            z = device // 8
+            at = slice(device * own_rows, (device + 1) * own_rows)
+            square_sends[place][z // 2, z % 2, y, x, core] = jnp.concatenate(
+                [result[at, :half], result[at, half:]], axis=0
+            ).astype(low)
+
+    get_mixture.wait()
+    square_pieces(0, dot(mixture_t[...], branch[...]))
+    square_sets[0].start()
+
+    square_loads[0].wait()
+    get_totals.wait()
+    for sentence in range(sentences):
+        spans = slice(sentence * slots, (sentence + 1) * slots)
+        result = dot(w_rows[0:width, :], branch[spans, :], 1, 1)
+        for head in range(heads):
+            at = slice(head * HD, (head + 1) * HD)
+            place = sentence * heads + head
+            value = result[at] * inverse_totals[place, 0:1, :]
+            mass = jnp.sum(value * mixture_t[at, spans].astype(full), axis=0, keepdims=True)
+            inverse_totals[place] = jnp.broadcast_to(mass, (8, slots))
+            inner_grad[sentence, at, 0:slots] = value.astype(low)
+    outer_set.step(2)
+
+    get_queries.wait()
+    get_keys.wait()
+    get_values.wait()
+    empty = jnp.zeros((HD, slots), low)
+    orders = heads * sentences
+    group_pairs = 2
+
+    def attend_back(step_index, carry):
+        pair = lax.div(step_index, sentences)
+        sentence = lax.rem(step_index, sentences)
+        start = pl.multiple_of(pair * 128, 128)
+        spans = pl.ds(pl.multiple_of(sentence * slots, slots), slots)
+        left = act[0, spans, pl.ds(start, 128)]
+        for half in range(2):
+            order = step_index * 2 + half
+            row = pl.multiple_of(start + half * HD, HD)
+            place = sentence * heads + pair * 2 + half
+            prob_copy(order).wait()
+
+            @pl.when(order + 3 < orders)
+            def _():
+                prob_copy(order + 3).start()
+
+            slot = lax.rem(order, 4)
+            prob = prob_slot(order)
+            upstream = inner_grad[sentence, pl.ds(row, HD), 0:slots]
+            right = jnp.concatenate(
+                [upstream, empty] if half == 0 else [empty, upstream], axis=0
+            )
+            toward = dot(left, right)
+            mass = inverse_totals[place, 0:1, :]
+            for piece in range(0, slots, 64):
+                score_grads[half, piece : piece + 64, :] = (
+                    prob[piece : piece + 64, :].astype(full) * (toward[piece : piece + 64] - mass)
+                ).astype(low)
+            value_grad = dot(upstream, prob[...], 1, 1)
+            key_spans = pl.ds(pl.multiple_of(rows + sentence * slots, slots), slots)
+            query = w_columns[pl.ds(row, HD), spans]
+            key = w_columns[pl.ds(row, HD), key_spans]
+            score = score_grads[half]
+            key_grad = dot(query, score, 1, 1)
+            query_grad = dot(key, score)
+            mixture_t[pl.ds(row, HD), spans] = value_grad.astype(low)
+            w_columns[pl.ds(row, HD), spans] = query_grad.astype(low)
+            w_columns[pl.ds(row, HD), key_spans] = key_grad.astype(low)
+        return carry
+
+    def projection_grads(group):
+        at = slice(group * 256, (group + 1) * 256)
+        results = []
+        for name in range(3):
+            total = None
+            for sentence in range(sentences):
+                left = inner_grad[2 + sentence, 0:width, 0:slots]
+                if name < 2:
+                    base = name * rows + sentence * slots
+                    right = w_columns[at, base : base + slots]
+                else:
+                    right = mixture_t[at, sentence * slots : (sentence + 1) * slots]
+                term = dot(left, right, 1, 1)
+                total = term if total is None else total + term
+            results.append(total * 0.125 if name == 0 else total)
+        square_pieces(1 + group, jnp.concatenate(results, axis=1))
+
+    def both(first, second):
+        first()
+        second()
+
+    ticks = {
+        0: {1: lambda: inner_set.step(1), 3: lambda: square_sets[0].step(0)},
+        1: {0: lambda: outer_set.step(3), 1: lambda: inner_set.step(2), 3: lambda: square_sets[0].step(1)},
+        2: {
+            0: lambda: both(
+                lambda: outer_set.step(4, outer_out), lambda: square_sets[1].step(0)
+            ),
+            1: lambda: inner_set.step(3),
+            2: lambda: square_sets[0].step(2),
+            3: lambda: square_sets[1].step(1),
+        },
+    }
+    for group in range(3):
+        steps = group_pairs * sentences
+
+        def group_step(index, carry, group=group):
+            attend_back(group * steps + index, 0)
+            for when, action in ticks[group].items():
+                pl.when(index == when)(action)
+            return carry
+
+        lax.fori_loop(0, steps, group_step, 0)
+        if group == 0:
+            for copy in get_tokens:
+                copy.wait()
+        projection_grads(group)
+        square_sets[1 + group].start()
+
+    ones = jnp.ones((8, rows), low)
+    vector_sums[6:7, :] = 0.125 * dot(ones, w_columns[:, 0:rows], 1, 1)[0:1, :]
+    vector_sums[7:8, :] = dot(ones, mixture_t[...], 1, 1)[0:1, :]
+
+    def sum_copy(stage):
+        return pltpu.make_async_remote_copy(
+            src_ref=sum_held.at[stage],
+            dst_ref=sum_recv.at[stage],
+            send_sem=sum_send.at[stage],
+            recv_sem=sum_sems.at[stage],
+            device_id=(links[("core", "x", "y", "z0", "z1")[stage]][1],),
+            device_id_type=pl.DeviceIdType.MESH,
+        )
+
+    def sum_step(stage):
+        sum_copy(stage).wait()
+        total = sum_held[stage] + sum_recv[stage]
+        if stage < 4:
+            sum_held[stage + 1] = total
+            sum_copy(stage + 1).start()
+        else:
+            sums_out[...] = total
+
+    sum_copy(0).start()
+    inner_set.step(4, inner_out)
+    square_sets[0].step(3)
+    square_sets[1].step(2)
+    square_sets[2].step(0)
+
+    for copy in square_loads[1:]:
+        copy.wait()
+
+    def token_block(sentence):
+        spans = slice(sentence * slots, (sentence + 1) * slots)
+        lefts = (
+            w_columns[:, spans],
+            w_columns[:, rows + sentence * slots : rows + (sentence + 1) * slots],
+            mixture_t[:, spans],
+        )
+        total = 0.125 * dot(lefts[0], w_rows[width : 2 * width, :], 0, 1)
+        total = total + dot(lefts[1], w_rows[2 * width : 3 * width, :], 0, 1)
+        total = total + dot(lefts[2], w_rows[3 * width : 4 * width, :], 0, 1)
+        grads[spans, :] = grads[spans, :] + total
+        return pltpu.make_async_copy(
+            grads.at[spans], token_grad_out.at[spans], load_sems.at[60 + sentence]
+        )
+
+    square_sets[3].step(0)
+    sum_step(0)
+    outs = []
+    for sentence in range(sentences):
+        copy = token_block(sentence)
+        copy.start()
+        outs.append(copy)
+        if sentence == 0:
+            square_sets[2].step(1)
+            square_sets[1].step(3)
+            square_sets[0].step(4, square_out.at[0])
+            square_sets[3].step(1)
+            sum_step(1)
+    square_sets[2].step(2)
+    square_sets[1].step(4, square_out.at[1])
+    square_sets[3].step(2)
+    sum_step(2)
+    square_sets[2].step(3)
+    square_sets[3].step(3)
+    sum_step(3)
+    square_sets[2].step(4, square_out.at[2])
+    square_sets[3].step(4, square_out.at[3])
+    sum_step(4)
+    for copy in outs:
+        copy.wait()
+
+
+def finish_kernel(
+    devices,
+    loss,
+    outer,
+    inner,
+    square,
+    sums,
+    loss_out,
+    query_out,
+    query_bias,
+    key_out,
+    value_out,
+    value_bias,
+    output_out,
+    output_bias,
+    first_gain,
+    first_shift,
+    inner_out,
+    inner_bias,
+    outer_out,
+    outer_bias,
+    second_gain,
+    second_shift,
+):
+    me = lax.axis_index("dp")
+    width = outer.shape[1]
+    own = query_out.shape[0]
+    loss_out[...] = loss[0:1, 0:1]
+    outer_out[...] = outer[...]
+    half = inner.shape[1]
+    inner_out[:, 0:half] = inner[0:own, :]
+    inner_out[:, half : 2 * half] = inner[own : 2 * own, :]
+    output_out[:, 0 : width // 2] = square[0, 0:own, :]
+    output_out[:, width // 2 : width] = square[0, own : 2 * own, :]
+    for group in range(3):
+        at = slice(group * 256, (group + 1) * 256)
+        first, second = square[1 + group, 0:own, :], square[1 + group, own : 2 * own, :]
+        query_out[:, at] = first[:, 0:256]
+        key_out[:, group * 256 : group * 256 + 128] = first[:, 256:384]
+        key_out[:, group * 256 + 128 : group * 256 + 256] = second[:, 0:128]
+        value_out[:, at] = second[:, 128:384]
+    source = lax.broadcasted_iota(jnp.int32, (width, 128), 0)
+    lane = lax.broadcasted_iota(jnp.int32, (width, 128), 1)
+
+    def pick(values, start):
+        chosen = jnp.where(source == lane + start, 1.0, 0.0)
+        return lax.dot_general(
+            values,
+            chosen,
+            (((1,), (0,)), ((), ())),
+            precision=lax.Precision.HIGHEST,
+            preferred_element_type=full,
+        )
+
+    picked = pick(sums[0:8, :], me * own)
+    for place, ref in enumerate(
+        (
+            outer_bias,
+            second_gain,
+            second_shift,
+            first_gain,
+            first_shift,
+            output_bias,
+            query_bias,
+            value_bias,
+        )
+    ):
+        ref[...] = picked[place : place + 1, 0 : ref.shape[1]]
+    wide = inner_bias.shape[1]
+    per_row = width // wide
+    row_ids = lax.broadcasted_iota(jnp.int32, (8, width), 0)
+    chosen = jnp.sum(
+        jnp.where(row_ids == lax.div(me, per_row), sums[8:16, :], 0.0), axis=0, keepdims=True
+    )
+    inner_bias[...] = pick(jnp.broadcast_to(chosen, (8, width)), lax.rem(me, per_row) * wide)[
+        0:1, 0:wide
+    ]
+
+
+def linked_device(
+    devices,
+    tokens,
+    lengths,
+    groups,
+    query_weight,
+    query_bias,
+    key_weight,
+    value_weight,
+    value_bias,
+    output_weight,
+    output_bias,
+    first_gain,
+    first_shift,
+    inner_weight,
+    inner_bias,
+    outer_weight,
+    outer_bias,
+    second_gain,
+    second_shift,
+):
+    sentences = lengths.shape[0]
+    rows, width = tokens.shape
+    slots = rows // sentences
+    inner = inner_weight.shape[1]
+    vectors = jnp.stack(
+        (
+            query_bias,
+            value_bias,
+            output_bias,
+            first_gain,
+            first_shift,
+            outer_bias,
+            second_gain,
+            second_shift,
+        )
+    )
+    weights = (query_weight, key_weight, value_weight, output_weight, inner_weight, outer_weight)
+    (
+        layer_output,
+        pooled,
+        live_mean,
+        queries_t,
+        keys_t,
+        values,
+        mixture_t,
+        probs,
+        inverse_totals,
+        first_normed,
+        first_inverse,
+        hidden_low,
+        second_normed,
+        second_inverse,
+        activated,
+        slopes,
+        tokens_t,
+    ) = forward(lengths, tokens, vectors, inner_bias[None], weights)
+    hbm = pl.BlockSpec(memory_space=pl.ANY)
+    vmem = pl.BlockSpec(memory_space=pltpu.VMEM)
+    shape = jax.ShapeDtypeStruct
+    piece_outer = (inner // devices, width)
+    piece_inner = (2 * width // devices, inner // 2)
+    piece_square = (2 * width // devices, width // 2)
+
+    def levels(piece, lead=()):
+        third = (piece[0] // 3, piece[1])
+        shapes = [(2,) * 5 + piece, (2,) * 4 + piece]
+        shapes += [(3,) + (2,) * k + third for k in (3, 2, 1, 0)]
+        return [pltpu.VMEM(lead + s, low) for s in shapes]
+
+    loss, token_grad, outer, inner_sum, square, sums = pl.pallas_call(
+        functools.partial(backward_kernel, devices, sentences),
+        in_specs=[vmem] * 4 + [hbm] * 20,
+        out_specs=[vmem, hbm, vmem, vmem, vmem, vmem],
+        out_shape=[
+            shape((8, 128), full),
+            shape((rows, width), full),
+            shape(piece_outer, full),
+            shape(piece_inner, full),
+            shape((4,) + piece_square, full),
+            shape((16, width), full),
+        ],
+        scratch_shapes=[
+            pltpu.VMEM(activated.shape, low),
+            pltpu.VMEM(activated.shape, low),
+            pltpu.VMEM((inner, width), low),
+            pltpu.VMEM((width, inner), low),
+            pltpu.VMEM((width, rows), low),
+            pltpu.VMEM((rows, width), full),
+            pltpu.VMEM((rows, width), full),
+            pltpu.VMEM((rows, width), low),
+            pltpu.VMEM((rows, width), low),
+            pltpu.VMEM((rows, 128), full),
+            pltpu.VMEM((rows, 128), full),
+            pltpu.VMEM(inverse_totals.shape, full),
+            pltpu.VMEM((2, slots, slots), low),
+            pltpu.VMEM((sentences, width), full),
+            pltpu.VMEM((devices, sentences, width), full),
+            pltpu.VMEM((devices * sentences, width), full),
+        ]
+        + levels(piece_outer)
+        + levels(piece_inner)
+        + levels(piece_square, (4,))[1:]
+        + [
+            pltpu.VMEM((5, 16, width), full),
+            pltpu.VMEM((5, 16, width), full),
+            pltpu.SemaphoreType.DMA((64,)),
+            pltpu.SemaphoreType.DMA((4,)),
+            pltpu.SemaphoreType.DMA((devices,)),
+            pltpu.SemaphoreType.DMA((devices,)),
+            pltpu.SemaphoreType.DMA((6, 5, 3)),
+            pltpu.SemaphoreType.DMA((6, 5, 3)),
+            pltpu.SemaphoreType.DMA((5,)),
+            pltpu.SemaphoreType.DMA((5,)),
+        ],
+        compiler_params=pltpu.CompilerParams(
+            collective_id=0, has_side_effects=True, vmem_limit_bytes=63 * MIB
+        ),
+        name="decode",
+    )(
+        pooled,
+        live_mean,
+        vectors,
+        groups.astype(full)[None],
+        activated,
+        slopes,
+        second_normed,
+        second_inverse,
+        hidden_low,
+        first_normed,
+        first_inverse,
+        mixture_t,
+        queries_t,
+        keys_t,
+        values,
+        tokens_t,
+        probs,
+        inverse_totals,
+        *weights,
+    )
+    own = width // devices
+    finals = pl.pallas_call(
+        functools.partial(finish_kernel, devices),
+        out_shape=[
+            shape((1, 1), full),
+            shape((own, width), full),
+            shape((1, own), full),
+            shape((own, width), full),
+            shape((own, width), full),
+            shape((1, own), full),
+            shape((own, width), full),
+            shape((1, own), full),
+            shape((1, own), full),
+            shape((1, own), full),
+            shape((own, inner), full),
+            shape((1, inner // devices), full),
+            shape((inner // devices, width), full),
+            shape((1, own), full),
+            shape((1, own), full),
+            shape((1, own), full),
+        ],
+        in_specs=[vmem] * 5,
+        out_specs=[vmem] * 16,
+        compiler_params=pltpu.CompilerParams(vmem_limit_bytes=32 * MIB),
+        name="finish",
+    )(loss, outer, inner_sum, square, sums)
+    finals = [f.reshape(f.shape[1:]) if f.shape[0] == 1 else f for f in finals]
+    return (finals[0].reshape(()), layer_output, token_grad, *finals[1:])
+
+
 highest = lax.Precision.HIGHEST
 
 
@@ -267,8 +1528,10 @@
         P(),
         P(),
     )
+    devices = mesh.shape["dp"]
+    body = functools.partial(linked_device, devices) if devices == 32 else per_device
     return jax.shard_map(
-        per_device,
+        body,
         mesh=mesh,
         in_specs=placed,
         out_specs=(

time: 1030 us -> 182 us (0.18)
  waiting for transfers between devices: 642 us -> 0 us
  matrix products: 165 us -> 0 us
  Pallas kernels: 0 us -> 165 us
  blocking collectives: 85.2 us -> 0 us
  local copies, waits for them, and re-layouts: 79.8 us -> 14.3 us
  other arithmetic: 37.5 us -> 1.17 us
  between operations: 15.2 us -> 0.69 us
    unnamed x11 -> x0, waiting for transfers between devices: 359 us -> none
    reduce_scatter x3 -> x0, waiting for transfers between devices: 283 us -> none  [the longest x1 142 us: per_device(): lax.psum_scatter(inner_weight_grad, 'dp', scatter_dimension=0, tiled=True)]
    pallas_call x0 -> x3, Pallas kernels: none -> 165 us  [the longest x1 107 us: linked_device(): pl.pallas_call(functools.partial(backward_kernel, devices, sentences), in...]
    dot_general x35 -> x0, matrix products: 165 us -> none  [the longest x6 51.3 us: project(): return jnp.dot(operand, weight, preferred_element_type=jnp.float32)]
    all_gather x1 -> x0, blocking collectives: 43.5 us -> none  [per_device(): lax.all_gather(pooled, 'dp', axis=0, tiled=True).astype(jnp.float32)]
    psum x1 -> x0, blocking collectives: 41.8 us -> none  [per_device(): loss_value = lax.psum(part_loss, 'dp')]
    while x48 -> x0, local copies, waits for them, and re-layouts: 24.8 us -> none  [the longest x4 11.4 us: per_device(): lax.map(attend, (head_queries, head_keys, head_values, key_live))]
    unnamed x174 -> x11, local copies, waits for them, and re-layouts: 27.3 us -> 8.11 us
  transfers between devices with their start and end apart: 7 -> 0, of which waited for: 6 -> 0; matrix products, arithmetic and copies ran while one was open for 12% -> 0% of each run, Pallas kernels for 0% -> 0%
where the time goes in v1:
time: 182 us
  Pallas kernels  165 us (91%)
  local copies, waits for them, and re-layouts  14.3 us (8%)
    pallas_call x1, Pallas kernels, linked_device(): pl.pallas_call(functools.partial(backward_kernel, devices, sentences), in...  107 us
    pallas_call x1, Pallas kernels, forward(): pl.pallas_call(forward_kernel, grid=(count,), in_specs=[pl.BlockSpec(memo...  56.8 us
    unnamed x11, local copies, waits for them, and re-layouts  8.11 us
    another operation x9, local copies, waits for them, and re-layouts, linked_device(): jnp.stack((query_bias, value_bias, output_bias, first_gain, first_shift,...  6.16 us

profile of v1, /device:TPU:0, one launch (start us, length us, event | category | flops | bytes accessed | tf_op | source)
XLA Modules:
  0.0 181.5 jit_solution(16043110087586605521)
XLA Ops:
  0.7 1.2 convert_bitcast_fusion.groups
  1.8 0.7 stack.27
  2.5 0.7 stack.28
  3.2 0.7 stack.29
  3.9 0.7 stack.30
  4.6 0.7 stack.31
  5.3 0.7 stack.32
  6.0 0.7 stack.33
  6.6 0.7 stack.34
  7.3 0.6 stack.35.vectors
  8.0 56.8 %encode.1 = (bf16[1024,768]{1,0:T(8,128)(2,1)}, f32[2,8,768]{2,1,0:T(8,128)}, f32[2,8,768]{2,1,0:T(8,128)}, bf16[768,1024]{1,0:T(8,128)(2,1)}, bf16[768,1024]{1,...) custom-call(s32[2]{0:T(128)} %lengths.1, ...), custom_call_target="tpu_custom_call" | custom-call | tf_op jit(solution)/shard_map/encode/pallas_call | solution.py:256
  64.8 107.3 %decode.1 = (f32[8,128]{1,0:T(8,128)}, f32[1024,768]{1,0:T(8,128)}, f32[96,768]{1,0:T(8,128)}, f32[48,1536]{1,0:T(8,128)}, f32[4,48,384]{2,1,0:T(8,128)}, /*index=5*/f32[16,768]{1,0:T(8,128)}) custom-call(f32[2,8,768]{2,1,0:T(8,128)} %get-tuple-element.57.pooled, f32[2,8,768]{2,1,0:T(8,128)} %get-tuple-element.58.live_mean, f32[8,768]{1,0:T(8,128)} %stack.35.vectors, ...), custom_call_target="tpu_custom_call" | custom-call | tf_op jit(solution)/shard_map/decode/pallas_call | solution.py:1176
  172.1 0.0 copy-start
  172.1 1.0 copy-done
  173.0 0.0 copy-start.1
  173.0 1.0 copy-done.1
  174.0 0.0 copy-start.2
  174.0 1.0 copy-done.2
  175.0 0.0 copy-start.3
  175.0 0.8 copy-done.3
  175.8 0.0 copy-start.4
  175.8 0.7 copy-done.4
  176.4 1.3 finish.1
  177.7 3.8 %copy.37 = f32[1024,768]{1,0:T(8,128)} copy(f32[1024,768]{1,0:T(8,128)} %get-tuple-element.116) | data formatting | bytes 6291456
Async XLA Ops:
  172.1 1.0 copy-start
  173.0 1.0 copy-start.1
  174.0 1.0 copy-start.2
  175.0 0.8 copy-start.3
  175.8 0.7 copy-start.4
